TPU v7x, 32 devices: a whole 2x2x4 slice. The times are simulated.
32 devices in a mesh: grp: 2 (over y), row: 4 (over z), col: 2 (over x), sub: 2 (over core).
Axes of the slice: x: 2, y: 2, z: 4, core: 2. Of those that a mesh axis runs over, the one named last changes fastest.
Arguments:
- samples: bfloat16 [512, 2, 16, 512], P(('grp', 'row', 'col', 'sub')), parts along dimension 0, may hold values from -6 to 6
- analysis_taps: float32 [16, 16], replicated, may hold values from -1 to 1
- synthesis_taps: float32 [16, 16], replicated, may hold values from -1 to 1
- antenna_station: int32 [512], P('grp'), parts along dimension 0, may hold values from 0 to 31, as said below
- station_group: int32 [64, 1], P('grp'), parts along dimension 0, may hold values from 0 to 7
- beam_group: int32 [2048], P('grp'), parts along dimension 0, may hold values from 0 to 7
- beam_weights: bfloat16 [32, 2, 1024, 32], P(('grp', 'row'), None, ('col', 'sub')), parts along dimension 0, may hold values from -6 to 6
Outputs:
- visibilities: float32 [16, 2, 64, 32], P('row', None, ('grp', 'col', 'sub')), parts along dimension 2
- beam_series: float32 [2048, 2, 16, 512], P(('grp', 'col', 'sub', 'row')), parts along dimension 0
There are 2 independent parts, one for each index of `grp`. A program takes and returns all parts, laid end to end along the dimension named above; an argument that names none is the same for every part. Nothing has to cross between parts.
Inputs may be any that keep to these rules, and one draw needn't show every extreme that they name: `antenna_station`: every station is named by exactly 8 antennas.
All inputs are finite; a program needn't handle non-finite values.
Results may differ from a plain program's by a relative error of at most 0.005.
Values may be sent and summed in bfloat16 or wider, within the bound.
A program may use at most 64 MiB of HBM per device.

v0:
```python
import math
import jax
import jax.numpy as jnp
from jax import lax
from jax.sharding import PartitionSpec as P

ANTENNAS_PER_STN = 8
SPEC = 512


def polyphase(signal, coefficients):
    length = signal.shape[-1]
    output = coefficients[0][:, None] * signal
    for tap_index in range(1, coefficients.shape[0]):
        shifted = jnp.pad(
            signal[..., : length - tap_index], [(0, 0)] * (signal.ndim - 1) + [(tap_index, 0)]
        )
        output = output + coefficients[tap_index][:, None] * shifted
    return output


def fourier_table(length, direction):
    indices = jnp.arange(length)
    angles = (
        2.0 * math.pi / length * (indices[:, None] * indices[None, :] % length).astype(jnp.float32)
    )
    cosine_part = jnp.cos(angles)
    sine_part = jnp.sin(angles)
    table = jnp.stack(
        [
            jnp.stack([cosine_part, direction * sine_part]),
            jnp.stack([-direction * sine_part, cosine_part]),
        ]
    )
    return table.transpose(0, 2, 1, 3) * (1.0 / math.sqrt(length))


def body(
    samples, analysis_taps, synthesis_taps, antenna_station, station_group, beam_group, beam_weights
):
    high = lax.Precision.HIGHEST
    block_count = lax.axis_size(("col", "sub"))
    block_index = lax.axis_index(("col", "sub"))
    filtered = polyphase(samples.astype(jnp.float32), analysis_taps)
    spectra = jnp.einsum(
        "aqcf,qcpk->apkf", filtered, fourier_table(samples.shape[2], -1.0), precision=high
    ).astype(jnp.bfloat16)
    turned = lax.all_to_all(spectra, "row", split_axis=2, concat_axis=0, tiled=True)
    local_count = spectra.shape[0]
    held_rows = turned.shape[0]
    chan_rows = turned.shape[2]
    spec_len = turned.shape[3]
    station_count = station_group.shape[0]
    flat_width = 2 * chan_rows * spec_len
    tile_rows = station_count // block_count
    shard_rows = lax.all_gather(turned, ("col", "sub"), axis=0, tiled=True)
    row_total = shard_rows.shape[0]
    positions = jnp.arange(row_total, dtype=jnp.int32)
    source_block = positions // held_rows
    offset_rows = positions % held_rows
    source_row = offset_rows // local_count
    antenna = offset_rows % local_count
    global_index = (source_row * block_count + source_block) * local_count + antenna
    targets = antenna_station[global_index]
    wanted = jnp.arange(station_count, dtype=jnp.int32)
    one_hot = (targets[None, :] == wanted[:, None]).astype(jnp.bfloat16)
    summed_values = jnp.dot(
        one_hot, shard_rows.reshape(row_total, flat_width), preferred_element_type=jnp.float32
    )
    flat_stations = (summed_values * (1.0 / math.sqrt(ANTENNAS_PER_STN))).astype(jnp.bfloat16)
    station_list = flat_stations.reshape(station_count, 2, chan_rows, spec_len)
    real_part = station_list[:, 0]
    imag_part = station_list[:, 1]
    own_rows = lax.dynamic_slice_in_dim(station_list, block_index * tile_rows, tile_rows, 0)
    own_real = own_rows[:, 0]
    own_imag = own_rows[:, 1]
    vis_real = (
        jnp.einsum("icf,jcf->cij", own_real, real_part, preferred_element_type=jnp.float32)
        + jnp.einsum("icf,jcf->cij", own_imag, imag_part, preferred_element_type=jnp.float32)
    ) * (1.0 / SPEC)
    vis_imag = (
        jnp.einsum("icf,jcf->cij", own_imag, real_part, preferred_element_type=jnp.float32)
        - jnp.einsum("icf,jcf->cij", own_real, imag_part, preferred_element_type=jnp.float32)
    ) * (1.0 / SPEC)
    visibilities = jnp.stack([vis_real, vis_imag], axis=1)
    beam_block = beam_weights.shape[2]
    own_groups = lax.dynamic_slice_in_dim(beam_group, block_index * beam_block, beam_block, 0)
    members = station_group[:, 0][None, :] == own_groups[:, None]
    scaling = 1.0 / jnp.sqrt(jnp.sum(members.astype(jnp.float32), axis=1))
    weights = jnp.where(members[None, None], beam_weights, jnp.zeros((), jnp.bfloat16))
    weight_real = weights[:, 0]
    imaginary_weight = weights[:, 1]
    beam_real = jnp.einsum(
        "cbs,scf->bcf", weight_real, real_part, preferred_element_type=jnp.float32
    ) - jnp.einsum("cbs,scf->bcf", imaginary_weight, imag_part, preferred_element_type=jnp.float32)
    beam_imag = jnp.einsum(
        "cbs,scf->bcf", weight_real, imag_part, preferred_element_type=jnp.float32
    ) + jnp.einsum("cbs,scf->bcf", imaginary_weight, real_part, preferred_element_type=jnp.float32)
    beams = (jnp.stack([beam_real, beam_imag], axis=1) * scaling[:, None, None, None]).astype(
        jnp.bfloat16
    )
    returned = lax.all_to_all(beams, "row", split_axis=0, concat_axis=2, tiled=True)
    inverse = jnp.einsum(
        "bqkf,qkpc->bpcf",
        returned.astype(jnp.float32),
        fourier_table(returned.shape[2], 1.0),
        precision=high,
    )
    beam_series = polyphase(inverse, synthesis_taps)
    return (visibilities, beam_series)


def solution(mesh):
    return jax.shard_map(
        body,
        mesh=mesh,
        in_specs=(
            P(("grp", "row", "col", "sub"), None, None, None),
            P(),
            P(),
            P("grp"),
            P("grp", None),
            P("grp"),
            P(("grp", "row"), None, ("col", "sub"), None),
        ),
        out_specs=(
            P("row", None, ("grp", "col", "sub"), None),
            P(("grp", "col", "sub", "row"), None, None, None),
        ),
        check_vma=False,
    )
```

profile of v0, /device:TPU:0, one launch (start us, length us, event | category | flops | bytes accessed | tf_op | source)
XLA Modules:
  0.0 157.8 jit_solution(14489460331540854039)
XLA Ops:
  7.4 1.2 slice.274
  8.5 1.2 slice.275
  11.6 5.1 %fusion.3 = bf16[16,2,16,512]{3,2,0,1:T(8,128)(2,1)S(1)} fusion(f32[16,2,16,497]{3,2,1,0:T(8,128)S(1)} %slice.288, f32[16,2,16,498]{3,2,1,0:T(8,128)S(1)} %slice.287, f32[16,2,16,499]{3,2,1,0:T(8,128)S(1)} %slice.286, f32[16,2,16,500]{3,2,1,0:T(8,128)S(1)} %slice.285, f32[16,2,16,501]{3,2,1,0:T(8,128)S(1)} %slice.284, f32[16,2,16,502]{3,2,1,0:T(8,128)S(1)} %slice.283, ...), kind=kOutput, calls=%fused_computation.11 | convolution fusion | flops 109316096 | bytes 16536576 | tf_op jit(solution)/shard_map/aqcf,qcpk->apkf/dot_general | solution.py:45
  17.1 20.6 %all_to_all.36 = bf16[16,2,16,512]{3,0,1,2:T(8,128)(2,1)S(1)} all-to-all(bf16[16,2,16,512]{3,0,1,2:T(8,128)(2,1)S(1)} %copy.55), channel_id=1, replica_groups=mesh['grp'=2,'row'=4,'col'=2,'sub'=2] {'row'}, dimensions={2} | all-to-all | bytes 1048576 | tf_op jit(solution)/shard_map/all_to_all | solution.py:48
  37.7 0.8 copy.57
  38.5 0.8 dynamic_slice.7
  39.4 1.9 %gather_fusion = s32[256]{0:T(256)S(1)} fusion(s32[256]{0:T(256)S(1)} %copy-done, s32[1024]{0:T(1024)S(1)} %pad_clamp_fusion), kind=kCustom, calls=%fused_computation | custom fusion | bytes 3072 | tf_op jit(solution)/shard_map/gather | solution.py:64
  41.5 18.9 %all-gather.2.cloned.1.call-done = bf16[256,2,4,512]{3,0,2,1:T(8,128)(2,1)} async-done(((bf16[64,2,4,512]{3,0,2,1:T(8,128)(2,1)}), bf16[256,2,4,512]{3,0,2,1:T(8,128)(2,1)}) %all-gather.2.cloned.1.call-update) | async-done | bytes 2097168 | tf_op jit(solution)/shard_map/all_gather | solution.py:56
  60.4 2.8 %copy.58 = bf16[256,2,4,512]{0,3,2,1:T(8,128)(2,1)S(1)} copy(bf16[256,2,4,512]{3,0,2,1:T(8,128)(2,1)} %all-gather.2.cloned.1.call-done) | data formatting | bytes 4194304 | tf_op jit(solution)/shard_map/all_gather | solution.py:56
  63.2 0.7 fusion
  64.2 0.5 fusion.72
  64.6 0.5 fusion.75
  65.1 0.5 subtract_bitcast_fusion
  65.6 0.5 add_bitcast_fusion
  66.6 3.1 %copy.64 = bf16[256,2,4,512]{3,2,1,0:T(4,128)(2,1)} copy(bf16[256,2,4,512]{0,3,2,1:T(8,128)(2,1)S(1)} %fusion.1) | data formatting | bytes 4194304 | tf_op jit(solution)/shard_map/convert_element_type | solution.py:99
  69.6 4.6 %all-to-all-start.1 = ((bf16[256,2,4,512]{3,2,1,0:T(4,128)(2,1)}), bf16[256,2,4,512]{3,2,1,0:T(4,128)(2,1)S(1)}, u32[]{:S(2)}, u32[]{:S(2)}) async-start(bf16[256,2,4,512]{3,2,1,0:T(4,128)(2,1)} %copy.64), calls=%async_computation.1 | async-start | bytes 4194304 | tf_op jit(solution)/shard_map/all_to_all | solution.py:102
  74.9 0.6 copy.67
  75.6 47.3 %all-to-all-done.1 = bf16[256,2,4,512]{3,2,1,0:T(4,128)(2,1)S(1)} async-done(((bf16[256,2,4,512]{3,2,1,0:T(4,128)(2,1)}), bf16[256,2,4,512]{3,2,1,0:T(4,128)(2,1)S(1)}, u32[]{:S(2)}, u32[]{:S(2)}) %all-to-all-start.1) | async-done | bytes 2097184 | tf_op jit(solution)/shard_map/all_to_all | solution.py:102
  122.8 0.7 copy.65
  123.5 2.9 %copy.66 = bf16[64,2,4,4,512]{4,3,2,1,0:T(4,128)(2,1)} copy(bf16[64,2,4,4,512]{4,0,2,3,1:T(8,128)(2,1)S(1)} %bitcast.188) | data formatting | bytes 4194304 | tf_op jit(solution)/shard_map/all_to_all | solution.py:102
  126.5 2.5 %reshape.302 = bf16[64,2,16,512,1]{3,2,1,0,4:T(8,128)(2,1)S(1)} reshape(bf16[64,2,4,4,512]{4,3,2,1,0:T(4,128)(2,1)} %copy.66) | data formatting | bytes 4194304 | tf_op jit(solution)/shard_map/all_to_all | solution.py:102
  129.0 2.0 %convolution_bitcast_fusion = f32[64,2,16,512]{3,2,0,1:T(8,128)S(1)} fusion(bf16[64,2,16,512,1]{3,2,1,0,4:T(8,128)(2,1)S(1)} %reshape.302, f32[1,2,16,16]{2,3,0,1:T(8,128)S(1)} %get-tuple-element.37, f32[1,2,16,16]{2,3,0,1:T(8,128)S(1)} %get-tuple-element.16), kind=kOutput, calls=%fused_computation.6 | convolution fusion | flops 402655232 | bytes 6295552 | tf_op jit(solution)/shard_map/bqkf,qkpc->bpcf/dot_general | solution.py:103
  131.0 17.3 %multiply_add_fusion = f32[64,2,16,512]{3,2,0,1:T(8,128)S(1)} fusion(f32[64,2,16,497]{3,2,0,1:T(8,128)S(1)} %bitcast.172, f32[64,2,16,498]{3,2,0,1:T(8,128)S(1)} %bitcast.173, f32[64,2,16,499]{3,2,0,1:T(8,128)S(1)} %bitcast.174, f32[64,2,16,500]{3,2,0,1:T(8,128)S(1)} %bitcast.175, f32[64,2,16,501]{3,2,0,1:T(8,128)S(1)} %bitcast.176, ...), kind=kLoop, calls=%fused_computation.5 | loop fusion | flops 32505856 | bytes 70321152 | tf_op jit(solution)/shard_map/add | solution.py:18
  148.4 2.6 %copy.68 = f32[64,2,16,512]{3,2,1,0:T(8,128)} copy(f32[64,2,16,512]{3,2,0,1:T(8,128)S(1)} %multiply_add_fusion) | data formatting | bytes 8388608
  (48 shorter events, 3.9 us)
Async XLA Ops:
  7.2 32.3 %copy-start = (s32[256]{0:T(256)S(1)}, s32[256]{0:T(256)}, u32[]{:S(2)}) copy-start(s32[256]{0:T(256)} %param.10) | copy-start | bytes 3076
  7.2 2.5 %copy-start.1 = (bf16[16,2,16,512]{3,2,1,0:T(8,128)(2,1)S(1)}, bf16[16,2,16,512]{3,2,1,0:T(8,128)(2,1)}, u32[]{:S(2)}) copy-start(bf16[16,2,16,512]{3,2,1,0:T(8,128)(2,1)} %param.7) | copy-start | bytes 1572868
  7.2 53.2 %all-gather.2.cloned.1.call-start = ((), (), s32[]{:S(2)}) async-start(), calls=%async_computation.2 | async-start | bytes 2621440 | tf_op jit(solution)/shard_map/all_gather | solution.py:56
  10.9 0.7 copy-start.3
  11.6 27.7 %copy-start.5 = (s32[32,1]{0,1:T(1,128)S(1)}, s32[32,1]{0,1:T(1,128)}, u32[]{:S(2)}) copy-start(s32[32,1]{0,1:T(1,128)} %param.11) | copy-start | bytes 388
  16.7 24.7 %copy-start.2 = (bf16[4,2,256,32]{2,3,1,0:T(8,128)(2,1)S(1)}, bf16[4,2,256,32]{2,3,1,0:T(8,128)(2,1)}, u32[]{:S(2)}) copy-start(bf16[4,2,256,32]{2,3,1,0:T(8,128)(2,1)} %param.13) | copy-start | bytes 393220
  66.5 7.7 %copy-start.4 = (f32[16,16]{1,0:T(8,128)S(1)}, f32[16,16]{1,0:T(8,128)}, u32[]{:S(2)}) copy-start(f32[16,16]{1,0:T(8,128)} %param.9) | copy-start | bytes 3076
  69.6 53.2 %all-to-all-start.1 = ((bf16[256,2,4,512]{3,2,1,0:T(4,128)(2,1)}), bf16[256,2,4,512]{3,2,1,0:T(4,128)(2,1)S(1)}, u32[]{:S(2)}, u32[]{:S(2)}) async-start(bf16[256,2,4,512]{3,2,1,0:T(4,128)(2,1)} %copy.64), calls=%async_computation.1 | async-start | bytes 4194304 | tf_op jit(solution)/shard_map/all_to_all | solution.py:102
Sparse Core Ops, SparseCore 0:
  38.6 21.6 all-gather.1
where the time goes:
time: 158 us
  waiting for transfers between devices  66.2 us (42%)
  local copies, waits for them, and re-layouts  23.5 us (15%)
  blocking collectives  20.6 us (13%)
  other arithmetic  18.1 us (11%)
  between operations  14.4 us (9%)
  matrix products  10.3 us (7%)
  starting transfers between devices  4.66 us (3%)
    all_to_all x1, waiting for transfers between devices, body(): lax.all_to_all(beams, 'row', split_axis=0, concat_axis=2, tiled=True)  47.3 us
    all_to_all x1, blocking collectives, body(): lax.all_to_all(spectra, 'row', split_axis=2, concat_axis=0, tiled=True)  20.6 us
    all_gather x1, waiting for transfers between devices, body(): shard_rows = lax.all_gather(turned, ('col', 'sub'), axis=0, tiled=True)  18.9 us
    add x1, other arithmetic, polyphase(): output = output + coefficients[tap_index][:, None] * shifted  17.3 us
    all_to_all x3, local copies, waits for them, and re-layouts, body(): lax.all_to_all(beams, 'row', split_axis=0, concat_axis=2, tiled=True)  6.19 us
    dot_general x1, matrix products, body(): jnp.einsum('aqcf,qcpk->apkf', filtered, fourier_table(samples.shape[2], -...  5.12 us
    all_to_all x1, starting transfers between devices, body(): lax.all_to_all(beams, 'row', split_axis=0, concat_axis=2, tiled=True)  4.62 us
    slice x15, local copies, waits for them, and re-layouts, polyphase(): signal[..., :length - tap_index]  3.91 us
  transfers between devices with their start and end apart: 2, of which 2 were waited for; matrix products, arithmetic and copies ran while one was open for 3% of the time, Pallas kernels for 0%

commit v1 on v0

--- a/solution.py
+++ b/solution.py
@@ -6,6 +6,13 @@
 
 ANTENNAS_PER_STN = 8
 SPEC = 512
+
+
+def switch_gates(panel, on_dim):
+    frame_out = list(panel.shape[1:])
+    frame_out[on_dim] *= panel.shape[0]
+    carry_out = jnp.moveaxis(panel, 0, on_dim).reshape(frame_out)
+    return carry_out
 
 
 def polyphase(signal, coefficients):
@@ -53,7 +60,27 @@
     station_count = station_group.shape[0]
     flat_width = 2 * chan_rows * spec_len
     tile_rows = station_count // block_count
-    shard_rows = lax.all_gather(turned, ("col", "sub"), axis=0, tiled=True)
+    nd = lax.axis_size(("col", "sub"))
+    block_list = []
+    for kk in range(nd):
+        block_list.append((kk, (kk + 1) % nd))
+    pages = []
+    for k0, dev_i in block_list:
+        pages.append((dev_i, k0))
+    heard, x_new = ([], [])
+    for b in range(nd - 1):
+        if b % 2 == 0:
+            current_value = lax.ppermute(heard[-1] if heard else turned, ("col", "sub"), block_list)
+            heard.append(current_value)
+        else:
+            after = lax.ppermute(x_new[-1] if x_new else turned, ("col", "sub"), pages)
+            x_new.append(after)
+    arr_out = jnp.stack([*heard[::-1], turned, *x_new], 0)
+    newest = lax.axis_index(("col", "sub"))
+    d_next = len(heard)
+    tile_out = newest - d_next
+    arr_out = arr_out[(jnp.arange(nd) - tile_out) % nd]
+    shard_rows = switch_gates(arr_out, 0)
     row_total = shard_rows.shape[0]
     positions = jnp.arange(row_total, dtype=jnp.int32)
     source_block = positions // held_rows

time: 158 us -> 147 us (0.930)
  between operations: 14.4 us -> 1.04 us
  local copies, waits for them, and re-layouts: 23.5 us -> 29.8 us
  waiting for transfers between devices: 66.2 us -> 61.2 us
    all_gather x1 -> x0, waiting for transfers between devices: 18.9 us -> none  [body(): shard_rows = lax.all_gather(turned, ('col', 'sub'), axis=0, tiled=True)]
    ppermute x0 -> x3, waiting for transfers between devices: none -> 15 us  [the longest x2 10.6 us: body(): lax.ppermute(heard[-1] if heard else turned, ('col', 'sub'), block_list)]
    gather x0 -> x2, local copies, waits for them, and re-layouts: none -> 6.55 us  [body(): arr_out = arr_out[(jnp.arange(nd) - tile_out) % nd]]
    another operation x0 -> x1, local copies, waits for them, and re-layouts: none -> 3.26 us  [body(): shard_rows.reshape(row_total, flat_width)]
    all_gather x1 -> x0, local copies, waits for them, and re-layouts: 2.77 us -> none  [body(): shard_rows = lax.all_gather(turned, ('col', 'sub'), axis=0, tiled=True)]
    ppermute x0 -> x3, starting transfers between devices: none -> 1.91 us  [the longest x1 1.77 us: body(): after = lax.ppermute(x_new[-1] if x_new else turned, ('col', 'sub'), pages)]
  transfers between devices with their start and end apart: 2 -> 4, of which waited for: 2 -> 4; matrix products, arithmetic and copies ran while one was open for 3% -> 3% of each run, Pallas kernels for 0% -> 0%
where the time goes in v1:
time: 147 us
  waiting for transfers between devices  61.2 us (42%)
  local copies, waits for them, and re-layouts  29.8 us (20%)
  blocking collectives  20.6 us (14%)
  other arithmetic  18.4 us (13%)
  matrix products  10.1 us (7%)
  starting transfers between devices  5.74 us (4%)
    all_to_all x1, waiting for transfers between devices, body(): lax.all_to_all(beams, 'row', split_axis=0, concat_axis=2, tiled=True)  46.2 us
    all_to_all x1, blocking collectives, body(): lax.all_to_all(spectra, 'row', split_axis=2, concat_axis=0, tiled=True)  20.6 us
    add x1, other arithmetic, polyphase(): output = output + coefficients[tap_index][:, None] * shifted  17.3 us
    ppermute x2, waiting for transfers between devices, body(): lax.ppermute(heard[-1] if heard else turned, ('col', 'sub'), block_list)  10.6 us
    gather x2, local copies, waits for them, and re-layouts, body(): arr_out = arr_out[(jnp.arange(nd) - tile_out) % nd]  6.55 us
    all_to_all x3, local copies, waits for them, and re-layouts, body(): lax.all_to_all(beams, 'row', split_axis=0, concat_axis=2, tiled=True)  6.19 us
    dot_general x1, matrix products, body(): jnp.einsum('aqcf,qcpk->apkf', filtered, fourier_table(samples.shape[2], -...  5.11 us
    ppermute x1, waiting for transfers between devices, body(): after = lax.ppermute(x_new[-1] if x_new else turned, ('col', 'sub'), pages)  4.39 us
  transfers between devices with their start and end apart: 4, of which 4 were waited for; matrix products, arithmetic and copies ran while one was open for 3% of the time, Pallas kernels for 0%

profile of v1, /device:TPU:0, one launch (start us, length us, event | category | flops | bytes accessed | tf_op | source)
XLA Modules:
  0.0 146.8 jit_solution(10426498056328943073)
XLA Ops:
  0.8 1.2 slice.276
  2.0 1.2 slice.277
  5.1 5.1 %fusion.3 = bf16[16,2,16,512]{3,2,0,1:T(8,128)(2,1)S(1)} fusion(f32[16,2,16,497]{3,2,1,0:T(8,128)S(1)} %slice.290, f32[16,2,16,498]{3,2,1,0:T(8,128)S(1)} %slice.289, f32[16,2,16,499]{3,2,1,0:T(8,128)S(1)} %slice.288, f32[16,2,16,500]{3,2,1,0:T(8,128)S(1)} %slice.287, f32[16,2,16,501]{3,2,1,0:T(8,128)S(1)} %slice.286, f32[16,2,16,502]{3,2,1,0:T(8,128)S(1)} %slice.285, ...), kind=kOutput, calls=%fused_computation.13 | convolution fusion | flops 109316096 | bytes 16536576 | tf_op jit(solution)/shard_map/aqcf,qcpk->apkf/dot_general | solution.py:52
  10.5 20.6 %all_to_all.36 = bf16[16,2,16,512]{3,0,1,2:T(8,128)(2,1)S(1)} all-to-all(bf16[16,2,16,512]{3,0,1,2:T(8,128)(2,1)S(1)} %copy.55), channel_id=1, replica_groups=mesh['grp'=2,'row'=4,'col'=2,'sub'=2] {'row'}, dimensions={2} | all-to-all | bytes 1048576 | tf_op jit(solution)/shard_map/all_to_all | solution.py:55
  31.2 0.8 dynamic_slice.7
  32.2 1.9 %gather_fusion = s32[256]{0:T(256)S(1)} fusion(s32[256]{0:T(256)S(1)} %copy-done, s32[1024]{0:T(1024)S(1)} %pad_clamp_fusion.1), kind=kCustom, calls=%fused_computation | custom fusion | bytes 3072 | tf_op jit(solution)/shard_map/gather | solution.py:91
  34.1 1.8 %collective-permute-start.2 = (bf16[64,2,4,512]{3,0,2,1:T(8,128)(2,1)S(1)}, bf16[64,2,4,512]{3,0,2,1:T(8,128)(2,1)S(1)}, u32[]{:S(2)}, u32[]{:S(2)}) collective-permute-start(bf16[64,2,4,512]{3,0,2,1:T(8,128)(2,1)S(1)} %bitcast.197), channel_id=1, source_target_pairs={{1,0},{2,1},{3,2},{0,3},{5,4},{6,5},{7,6},{4,7},{9,8},{10,9},{11,1... | collective-permute-start | bytes 1572872 | tf_op jit(solution)/shard_map/ppermute | solution.py:76
  35.9 4.8 %collective-permute-done = bf16[64,2,4,512]{3,0,2,1:T(8,128)(2,1)S(1)} collective-permute-done((bf16[64,2,4,512]{3,0,2,1:T(8,128)(2,1)S(1)}, bf16[64,2,4,512]{3,0,2,1:T(8,128)(2,1)S(1)}, u32[]{:S(2)}, u32[]{:S(2)}) %collective-permute-start) | collective-permute-done | bytes 524320 | tf_op jit(solution)/shard_map/ppermute | solution.py:73
  40.9 4.4 %collective-permute-done.2 = bf16[64,2,4,512]{3,0,2,1:T(8,128)(2,1)S(1)} collective-permute-done((bf16[64,2,4,512]{3,0,2,1:T(8,128)(2,1)S(1)}, bf16[64,2,4,512]{3,0,2,1:T(8,128)(2,1)S(1)}, u32[]{:S(2)}, u32[]{:S(2)}) %collective-permute-start.2) | collective-permute-done | bytes 524320 | tf_op jit(solution)/shard_map/ppermute | solution.py:76
  45.2 5.8 %collective-permute-done.1 = bf16[64,2,4,512]{3,0,2,1:T(8,128)(2,1)S(1)} collective-permute-done((bf16[64,2,4,512]{3,0,2,1:T(8,128)(2,1)S(1)}, bf16[64,2,4,512]{3,0,2,1:T(8,128)(2,1)S(1)}, u32[]{:S(2)}, u32[]{:S(2)}) %collective-permute-start.1) | collective-permute-done | bytes 524320 | tf_op jit(solution)/shard_map/ppermute | solution.py:73
  51.3 2.0 %gather_fusion.1 = bf16[4,64,2,4,512]{4,1,3,2,0:T(8,128)(2,1)} fusion(bf16[4,64,2,4,512]{4,1,3,2,0:T(8,128)(2,1)S(1)} %pad_maximum_fusion, s32[1024]{0:T(1024)S(1)} %pad_clamp_fusion), kind=kCustom, calls=%fused_computation.1 | custom fusion | bytes 4194320 | tf_op jit(solution)/shard_map/gather | solution.py:82
  53.3 4.5 %copy.59 = bf16[4,64,2,4,512]{4,3,2,1,0:T(4,128)(2,1)} copy(bf16[4,64,2,4,512]{4,1,3,2,0:T(8,128)(2,1)} %gather_fusion.1) | data formatting | bytes 4194304 | tf_op jit(solution)/shard_map/gather | solution.py:82
  57.9 3.3 %reshape_reshape.3 = bf16[256,4096]{1,0:T(8,128)(2,1)S(1)} reshape(bf16[4,64,2,4,512]{4,3,2,1,0:T(4,128)(2,1)} %copy.59) | data formatting | bytes 4194304 | tf_op jit(solution)/shard_map/reshape;reshape | solution.py:95
  62.9 0.5 subtract_bitcast_fusion
  64.3 3.1 %copy.65 = bf16[256,2,4,512]{3,2,1,0:T(4,128)(2,1)} copy(bf16[256,2,4,512]{0,3,2,1:T(8,128)(2,1)S(1)} %fusion.1) | data formatting | bytes 4194304 | tf_op jit(solution)/shard_map/convert_element_type | solution.py:126
  67.4 3.8 %all-to-all-start.1 = ((bf16[256,2,4,512]{3,2,1,0:T(4,128)(2,1)}), bf16[256,2,4,512]{3,2,1,0:T(4,128)(2,1)S(1)}, u32[]{:S(2)}, u32[]{:S(2)}) async-start(bf16[256,2,4,512]{3,2,1,0:T(4,128)(2,1)} %copy.65), calls=%async_computation.1 | async-start | bytes 4194304 | tf_op jit(solution)/shard_map/all_to_all | solution.py:129
  71.9 0.6 copy.68
  72.6 46.2 %all-to-all-done.1 = bf16[256,2,4,512]{3,2,1,0:T(4,128)(2,1)S(1)} async-done(((bf16[256,2,4,512]{3,2,1,0:T(4,128)(2,1)}), bf16[256,2,4,512]{3,2,1,0:T(4,128)(2,1)S(1)}, u32[]{:S(2)}, u32[]{:S(2)}) %all-to-all-start.1) | async-done | bytes 2097184 | tf_op jit(solution)/shard_map/all_to_all | solution.py:129
  118.7 0.7 copy.66
  119.4 2.9 %copy.67 = bf16[64,2,4,4,512]{4,3,2,1,0:T(4,128)(2,1)} copy(bf16[64,2,4,4,512]{4,0,2,3,1:T(8,128)(2,1)S(1)} %bitcast.194) | data formatting | bytes 4194304 | tf_op jit(solution)/shard_map/all_to_all | solution.py:129
  122.4 2.5 %reshape.356 = bf16[64,2,16,512,1]{3,2,1,0,4:T(8,128)(2,1)S(1)} reshape(bf16[64,2,4,4,512]{4,3,2,1,0:T(4,128)(2,1)} %copy.67) | data formatting | bytes 4194304 | tf_op jit(solution)/shard_map/all_to_all | solution.py:129
  124.9 2.0 %convolution_bitcast_fusion = f32[64,2,16,512]{3,2,0,1:T(8,128)S(1)} fusion(bf16[64,2,16,512,1]{3,2,1,0,4:T(8,128)(2,1)S(1)} %reshape.356, f32[1,2,16,16]{2,3,0,1:T(8,128)S(1)} %get-tuple-element.37, f32[1,2,16,16]{2,3,0,1:T(8,128)S(1)} %get-tuple-element.16), kind=kOutput, calls=%fused_computation.7 | convolution fusion | flops 402655232 | bytes 6295552 | tf_op jit(solution)/shard_map/bqkf,qkpc->bpcf/dot_general | solution.py:130
  126.9 17.3 %multiply_add_fusion = f32[64,2,16,512]{3,2,0,1:T(8,128)S(1)} fusion(f32[64,2,16,497]{3,2,0,1:T(8,128)S(1)} %bitcast.179, f32[64,2,16,498]{3,2,0,1:T(8,128)S(1)} %bitcast.180, f32[64,2,16,499]{3,2,0,1:T(8,128)S(1)} %bitcast.181, f32[64,2,16,500]{3,2,0,1:T(8,128)S(1)} %bitcast.182, f32[64,2,16,501]{3,2,0,1:T(8,128)S(1)} %bitcast.183, ...), kind=kLoop, calls=%fused_computation.6 | loop fusion | flops 32505856 | bytes 70321152 | tf_op jit(solution)/shard_map/add | solution.py:25
  144.3 2.6 %copy.69 = f32[64,2,16,512]{3,2,1,0:T(8,128)} copy(f32[64,2,16,512]{3,2,0,1:T(8,128)S(1)} %multiply_add_fusion) | data formatting | bytes 8388608
  (56 shorter events, 6.2 us)
Async XLA Ops:
  0.6 31.5 %copy-start = (s32[256]{0:T(256)S(1)}, s32[256]{0:T(256)}, u32[]{:S(2)}) copy-start(s32[256]{0:T(256)} %param.10) | copy-start | bytes 3076
  0.6 2.5 %copy-start.1 = (bf16[16,2,16,512]{3,2,1,0:T(8,128)(2,1)S(1)}, bf16[16,2,16,512]{3,2,1,0:T(8,128)(2,1)}, u32[]{:S(2)}) copy-start(bf16[16,2,16,512]{3,2,1,0:T(8,128)(2,1)} %param.7) | copy-start | bytes 1572868
  4.4 0.7 copy-start.3
  5.1 26.9 %copy-start.5 = (s32[32,1]{0,1:T(1,128)S(1)}, s32[32,1]{0,1:T(1,128)}, u32[]{:S(2)}) copy-start(s32[32,1]{0,1:T(1,128)} %param.11) | copy-start | bytes 388
  10.2 30.6 %copy-start.2 = (bf16[4,2,256,32]{2,3,1,0:T(8,128)(2,1)S(1)}, bf16[4,2,256,32]{2,3,1,0:T(8,128)(2,1)}, u32[]{:S(2)}) copy-start(bf16[4,2,256,32]{2,3,1,0:T(8,128)(2,1)} %param.13) | copy-start | bytes 393220
  31.2 9.5 %collective-permute-start = (bf16[64,2,4,512]{3,0,2,1:T(8,128)(2,1)S(1)}, bf16[64,2,4,512]{3,0,2,1:T(8,128)(2,1)S(1)}, u32[]{:S(2)}, u32[]{:S(2)}) collective-permute-start(bf16[64,2,4,512]{3,0,2,1:T(8,128)(2,1)S(1)} %bitcast.196), channel_id=1, source_target_pairs={{0,1},{1,2},{2,3},{3,0},{4,5},{5,6},{6,7},{7,4},{8,9},{9,10},{10,1... | collective-permute-start | bytes 1572872 | tf_op jit(solution)/shard_map/ppermute | solution.py:73
  34.1 11.1 %collective-permute-start.2 = (bf16[64,2,4,512]{3,0,2,1:T(8,128)(2,1)S(1)}, bf16[64,2,4,512]{3,0,2,1:T(8,128)(2,1)S(1)}, u32[]{:S(2)}, u32[]{:S(2)}) collective-permute-start(bf16[64,2,4,512]{3,0,2,1:T(8,128)(2,1)S(1)} %bitcast.197), channel_id=1, source_target_pairs={{1,0},{2,1},{3,2},{0,3},{5,4},{6,5},{7,6},{4,7},{9,8},{10,9},{11,1... | collective-permute-start | bytes 1572872 | tf_op jit(solution)/shard_map/ppermute | solution.py:76
  40.7 10.4 %collective-permute-start.1 = (bf16[64,2,4,512]{3,0,2,1:T(8,128)(2,1)S(1)}, bf16[64,2,4,512]{3,0,2,1:T(8,128)(2,1)S(1)}, u32[]{:S(2)}, u32[]{:S(2)}) collective-permute-start(bf16[64,2,4,512]{3,0,2,1:T(8,128)(2,1)S(1)} %collective-permute-done), channel_id=1, source_target_pairs={{0,1},{1,2},{2,3},{3,0},{4,5},{5,6},{6,7},{7,4},{8,9},{9,10},{10,1... | collective-permute-start | bytes 1572872 | tf_op jit(solution)/shard_map/ppermute | solution.py:73
  64.3 6.9 %copy-start.4 = (f32[16,16]{1,0:T(8,128)S(1)}, f32[16,16]{1,0:T(8,128)}, u32[]{:S(2)}) copy-start(f32[16,16]{1,0:T(8,128)} %param.9) | copy-start | bytes 3076
  67.4 51.3 %all-to-all-start.1 = ((bf16[256,2,4,512]{3,2,1,0:T(4,128)(2,1)}), bf16[256,2,4,512]{3,2,1,0:T(4,128)(2,1)S(1)}, u32[]{:S(2)}, u32[]{:S(2)}) async-start(bf16[256,2,4,512]{3,2,1,0:T(4,128)(2,1)} %copy.65), calls=%async_computation.1 | async-start | bytes 4194304 | tf_op jit(solution)/shard_map/all_to_all | solution.py:129
